TPU v7x, 32 devices: a whole 2x2x4 slice. The times are simulated.
32 devices in a mesh: dp: 2 (over x), dom: 16 (over z, y, core).
Axes of the slice: x: 2, y: 2, z: 4, core: 2. Of those that a mesh axis runs over, the one named last changes fastest.
Arguments:
- features: bfloat16 [2, 16384, 256], P('dp', 'dom'), may hold values from -6 to 6
- send_order: int32 [16, 1024], P('dom'), may hold values from 0 to 1023, each once within a row
- adj_count: int32 [128], P('dom'), may hold values from 2 to 4, as said below
- adj_target: int32 [128, 4], P('dom'), may hold values from 6 to 17, as said below
- adj_vals: bfloat16 [128, 4, 128, 128], P('dom'), may hold values from -0.3125 to 0.3125
- w_edge: bfloat16 [256, 256], replicated, may hold values from -0.375 to 0.375
- w_node: bfloat16 [512, 256], replicated, may hold values from -0.25 to 0.25
- cotangent: bfloat16 [2, 16384, 256], P('dp', 'dom'), may hold values from -6 to 6
Outputs:
- node_out: bfloat16 [2, 16384, 256], P('dp', 'dom')
- grad_features: bfloat16 [2, 16384, 256], P('dp', 'dom')
- grad_edge: float32 [256, 256], replicated
- grad_node: float32 [512, 256], replicated
Inputs may be any that keep to these rules, and one draw needn't show every extreme that they name: Each row of send_order is a permutation of 0 to 1023. `adj_count`: every partition has its own most count, reached by one of its blocks; some partition's most is 4. `adj_target`: targets lie in the own partition's blocks or in the last 2 blocks of the previous partition or the first 2 blocks of the next one; slot 0 of each partition's first column block targets the previous partition, and slot 1 of its last column block targets the next one.
All inputs are finite; a program needn't handle non-finite values.
Results may differ from a plain program's by a relative error of at most 0.009.
Values may be sent and summed in bfloat16 or wider, within the bound.
No kernel may reach another device: no remote copies, remote signals or barrier semaphores. Data moves between devices by JAX's collectives and lax.ppermute only.
A program may use at most 64 MiB of HBM per device.

v0:
```python
import math

import jax
import jax.numpy as jnp
from jax import lax
from jax.sharding import PartitionSpec as P


def passed_along(x, axis, by):
    peers = lax.axis_size(axis)
    return lax.ppermute(x, axis, [(i, (i + by) % peers) for i in range(peers)])


def dsilu(value):
    sig = jax.nn.sigmoid(value)
    return sig * (1.0 + value * (1.0 - sig))


def shards(features, send_order, adj_count, adj_target, adj_vals, w_edge, w_node, cotangent):
    ndom = lax.axis_size("dom")
    rows = features.shape[1]
    width = features.shape[2]
    per_peer = rows // ndom
    blocks = rows // 128
    slots = adj_target.shape[1]
    order = send_order[0]
    picked = jnp.take(features[0], order, axis=0).reshape(ndom, per_peer, width)
    nodes = lax.all_to_all(picked, "dom", split_axis=0, concat_axis=0, tiled=True).reshape(
        rows, width
    )
    pre_edge = jnp.dot(nodes, w_edge, preferred_element_type=jnp.float32)
    message = jax.nn.silu(pre_edge).astype(jnp.bfloat16)
    msg_blocks = message.reshape(blocks, 128, width)
    wins = jnp.arange(3 * blocks, dtype=jnp.int32)
    live = jnp.arange(slots, dtype=jnp.int32)[None, :] < adj_count[:, None]
    table = (adj_target[None, :, :] == wins[:, None, None]) & live[None]
    table_f = table.astype(jnp.float32)
    table_b = table.astype(jnp.bfloat16)
    contrib = jnp.einsum("csrk,ckh->csrh", adj_vals, msg_blocks, preferred_element_type=jnp.float32)
    window = jnp.einsum("wcs,csrh->wrh", table_f, contrib, precision=lax.Precision.HIGHEST)
    window_b = window.astype(jnp.bfloat16)
    send_prev = window_b[:blocks]
    send_next = window_b[2 * blocks :]
    from_next = passed_along(send_prev, "dom", -1)
    from_prev = passed_along(send_next, "dom", 1)
    agg = (
        window_b[blocks : 2 * blocks].astype(jnp.float32)
        + from_next.astype(jnp.float32)
        + from_prev.astype(jnp.float32)
    )
    aggregate = agg.astype(jnp.bfloat16).reshape(rows, width)
    joined = jnp.concatenate([nodes, aggregate], axis=1)
    pre_node = jnp.dot(joined, w_node, preferred_element_type=jnp.float32)
    node_out = (nodes.astype(jnp.float32) + jax.nn.silu(pre_node)).astype(jnp.bfloat16)
    gout = cotangent[0].astype(jnp.float32)
    d_node = (gout * dsilu(pre_node)).astype(jnp.bfloat16)
    back = jnp.einsum("nh,dh->nd", d_node, w_node, preferred_element_type=jnp.float32)
    d_nodes1 = gout + back[:, :width]
    d_agg = back[:, width:].astype(jnp.bfloat16).reshape(blocks, 128, width)
    prev_rows = passed_along(d_agg, "dom", 1)
    next_rows = passed_along(d_agg, "dom", -1)
    window_g = jnp.concatenate([prev_rows, d_agg, next_rows], axis=0)
    gathered = jnp.einsum(
        "wcs,wrh->csrh", table_b, window_g, preferred_element_type=jnp.float32
    ).astype(jnp.bfloat16)
    d_message = jnp.einsum("csrk,csrh->ckh", adj_vals, gathered, preferred_element_type=jnp.float32)
    d_message = d_message.astype(jnp.bfloat16).reshape(rows, width)
    d_edge = (d_message.astype(jnp.float32) * dsilu(pre_edge)).astype(jnp.bfloat16)
    d_nodes = (
        d_nodes1 + jnp.einsum("nh,dh->nd", d_edge, w_edge, preferred_element_type=jnp.float32)
    ).astype(jnp.bfloat16)
    returned = lax.all_to_all(
        d_nodes.reshape(ndom, per_peer, width), "dom", split_axis=0, concat_axis=0, tiled=True
    ).reshape(rows, width)
    grad_brick = jnp.zeros_like(returned).at[order].set(returned)
    local_edge = jnp.einsum("nd,nh->dh", nodes, d_edge, preferred_element_type=jnp.float32)
    local_node = jnp.einsum("nd,nh->dh", joined, d_node, preferred_element_type=jnp.float32)
    scale = 1.0 / math.sqrt(float(lax.axis_size("dp") * rows * ndom))
    stacked = jnp.concatenate([local_edge, local_node], axis=0)
    share = lax.psum_scatter(stacked, "dom", scatter_dimension=0, tiled=True)
    share = lax.psum(share, "dp")
    whole = lax.all_gather(share, "dom", axis=0, tiled=True)
    grad_edge = whole[:width]
    grad_node = whole[width:]
    return (node_out[None], grad_brick[None], grad_edge * scale, grad_node * scale)


def solution(mesh):
    in_specs = (
        P("dp", "dom", None),
        P("dom", None),
        P("dom"),
        P("dom", None),
        P("dom", None, None, None),
        P(),
        P(),
        P("dp", "dom", None),
    )
    out_specs = (P("dp", "dom", None), P("dp", "dom", None), P(), P())
    return jax.shard_map(shards, mesh=mesh, in_specs=in_specs, out_specs=out_specs, check_vma=False)
```

profile of v0, /device:TPU:0, one launch (start us, length us, event | category | flops | bytes accessed | tf_op | source)
XLA Modules:
  0.0 183.1 jit_solution(12063817404780016690)
XLA Ops:
  7.2 0.0 copy-start
  7.2 0.8 compare_select_fusion
  8.0 0.5 broadcast.53
  8.5 1.3 reduce.3
  9.8 0.1 squeeze.9
  9.9 4.6 %gather_fusion = bf16[1024,256]{1,0:T(8,128)(2,1)S(1)} fusion(bf16[1024,256]{1,0:T(8,128)(2,1)} %bitcast.66, s32[1024]{0:T(1024)S(1)} %broadcast_clamp_fusion), kind=kCustom, calls=%fused_computation | custom fusion | bytes 1052672 | tf_op jit(solution)/shard_map/jit(_take)/gather | solution.py:27
  14.5 0.0 copy-start.9
  14.5 0.0 copy-start.7
  14.5 1.0 broadcast_select_fusion
  15.5 7.4 %all-to-all-start = ((bf16[16,64,256]{2,1,0:T(8,128)(2,1)}), bf16[16,64,256]{2,1,0:T(8,128)(2,1)S(1)}, u32[]{:S(2)}, u32[]{:S(2)}) async-start(bf16[16,64,256]{2,1,0:T(8,128)(2,1)} %broadcast_select_fusion), calls=%async_computation | async-start | bytes 1048576 | tf_op jit(solution)/shard_map/all_to_all | solution.py:28
  22.9 0.0 reduce-scatter.2.cloned.1.call-start
  23.0 0.0 copy-done.9
  23.0 14.4 %all-to-all-done = bf16[16,64,256]{2,1,0:T(8,128)(2,1)S(1)} async-done(((bf16[16,64,256]{2,1,0:T(8,128)(2,1)}), bf16[16,64,256]{2,1,0:T(8,128)(2,1)S(1)}, u32[]{:S(2)}, u32[]{:S(2)}) %all-to-all-start) | async-done | bytes 524320 | tf_op jit(solution)/shard_map/all_to_all | solution.py:28
  37.4 0.0 copy-start.2
  37.4 0.0 copy-done.7
  37.4 1.4 multiply_convert_fusion
  38.8 0.0 copy-done
  38.8 2.7 %fusion.30 = f32[8,256,4,128]{3,1,2,0:T(8,128)} fusion(bf16[8,128,256,1]{2,1,3,0:T(8,128)(2,1)S(1)} %bitcast.80, bf16[8,4,128,128]{3,2,1,0:T(8,128)(2,1)S(1)} %copy-done), kind=kOutput, calls=%fused_computation.52 | convolution fusion | flops 268435456 | bytes 5767168 | tf_op jit(solution)/shard_map/csrk,ckh->csrh/dot_general | solution.py:39
  41.5 0.0 copy-start.8
  41.5 5.5 %copy.17 = f32[8,256,4,128]{1,0,2,3:T(8,128)} copy(f32[8,256,4,128]{3,1,2,0:T(8,128)} %fusion.30) | data formatting | bytes 8388608 | tf_op jit(solution)/shard_map/csrk,ckh->csrh/dot_general | solution.py:39
  47.0 0.0 copy-done.8
  47.0 4.2 %bitcast_convert_fusion = bf16[24,128,256]{2,0,1:T(8,128)(2,1)S(1)} fusion(f32[8,256,4,128]{1,0,2,3:T(8,128)} %copy.17, s32[8,4]{0,1:T(4,128)S(1)} %copy-done.8, pred[8,4]{0,1:T(4,128)(4,1)S(1)} %iota_compare_fusion.1), kind=kOutput, calls=%fused_computation.5 | convolution fusion | flops 302777856 | bytes 5767328 | tf_op jit(solution)/shard_map/wcs,csrh->wrh/dot_general | solution.py:40
  51.2 0.1 fusion.29
  51.3 0.0 copy-start.5
  51.3 0.0 copy-start.6
  51.3 2.7 %collective-permute-start = (bf16[8,128,256]{2,0,1:T(8,128)(2,1)S(1)}, bf16[8,128,256]{2,0,1:T(8,128)(2,1)S(1)}, u32[]{:S(2)}, u32[]{:S(2)}) collective-permute-start(bf16[8,128,256]{2,0,1:T(8,128)(2,1)S(1)} %get-tuple-element.4), channel_id=1, source_target_pairs={{0,15},{1,0},{2,1},{3,2},{4,3},{5,4},{6,5},{7,6},{8,7},{9,8},{10,9... | collective-permute-start | bytes 1572872 | tf_op jit(solution)/shard_map/ppermute | solution.py:11
  54.0 0.0 collective-permute-start.1
  54.0 6.7 %collective-permute-done = bf16[8,128,256]{2,0,1:T(8,128)(2,1)S(1)} collective-permute-done((bf16[8,128,256]{2,0,1:T(8,128)(2,1)S(1)}, bf16[8,128,256]{2,0,1:T(8,128)(2,1)S(1)}, u32[]{:S(2)}, u32[]{:S(2)}) %collective-permute-start) | collective-permute-done | bytes 524320 | tf_op jit(solution)/shard_map/ppermute | solution.py:11
  60.7 4.7 %collective-permute-done.1 = bf16[8,128,256]{2,0,1:T(8,128)(2,1)S(1)} collective-permute-done((bf16[8,128,256]{2,0,1:T(8,128)(2,1)S(1)}, bf16[8,128,256]{2,0,1:T(8,128)(2,1)S(1)}, u32[]{:S(2)}, u32[]{:S(2)}) %collective-permute-start.1) | collective-permute-done | bytes 524320 | tf_op jit(solution)/shard_map/ppermute | solution.py:11
  65.4 0.2 add_convert_fusion.1
  65.6 0.1 copy.14
  65.7 0.0 copy-done.2
  65.7 0.0 copy-done.5
  65.7 0.0 copy-done.6
  65.7 1.5 fusion.11
  67.2 0.0 copy-start.3
  67.2 0.5 fusion.31
  67.7 0.1 slice.43
  67.8 0.3 collective-permute-start.2
  68.1 4.2 %collective-permute-start.3 = (bf16[8,128,256]{2,1,0:T(8,128)(2,1)S(1)}, bf16[8,128,256]{2,1,0:T(8,128)(2,1)S(1)}, u32[]{:S(2)}, u32[]{:S(2)}) collective-permute-start(bf16[8,128,256]{2,1,0:T(8,128)(2,1)S(1)} %bitcast.72), channel_id=1, source_target_pairs={{0,15},{1,0},{2,1},{3,2},{4,3},{5,4},{6,5},{7,6},{8,7},{9,8},{10,9... | collective-permute-start | bytes 1572872 | tf_op jit(solution)/shard_map/ppermute | solution.py:11
  72.3 0.0 copy-done.3
  72.3 0.5 fusion.13
  72.8 6.5 %collective-permute-done.2 = bf16[8,128,256]{2,1,0:T(8,128)(2,1)S(1)} collective-permute-done((bf16[8,128,256]{2,1,0:T(8,128)(2,1)S(1)}, bf16[8,128,256]{2,1,0:T(8,128)(2,1)S(1)}, u32[]{:S(2)}, u32[]{:S(2)}) %collective-permute-start.2) | collective-permute-done | bytes 524320 | tf_op jit(solution)/shard_map/ppermute | solution.py:11
  79.2 0.0 collective-permute-done.3
  79.2 0.2 maximum_bitcast_fusion
  79.4 1.3 fusion.5
  80.7 0.0 copy-start.4
  80.7 0.8 fusion.10
  81.6 0.4 copy-done.4
  82.0 0.4 fusion.12
  82.3 0.0 copy-start.1
  82.3 0.8 copy-done.1
  83.1 0.3 fusion.32
  83.5 0.9 pad_maximum_fusion.1
  84.4 0.0 reduce-scatter.2.cloned.1.call-update
  84.4 1.5 fusion.8
  86.0 21.7 %all_to_all.10 = bf16[16,64,256]{2,1,0:T(8,128)(2,1)S(1)} all-to-all(bf16[16,64,256]{2,1,0:T(8,128)(2,1)S(1)} %bitcast.74), channel_id=1, replica_groups=mesh['dp'=2,'dom'=16] {'dom'}, dimensions={0} | all-to-all | bytes 1048576 | tf_op jit(solution)/shard_map/all_to_all | solution.py:72
  107.6 5.7 %scatter_custom_fusion = bf16[1024,256]{1,0:T(8,128)(2,1)} fusion(s32[1024]{0:T(1024)S(1)} %bitcast.82, bf16[1024,256]{1,0:T(8,128)(2,1)S(1)} %bitcast.79, bf16[]{:T(256)} %constant.26.clone.1), kind=kCustom, calls=%fused_computation.34 | custom fusion | bytes 524290 | tf_op jit(solution)/shard_map/scatter | solution.py:75
  113.4 30.5 %reduce-scatter.2.cloned.1.call-done = f32[48,256]{1,0:T(8,128)} async-done(((f32[768,256]{1,0:T(8,128)}), f32[48,256]{1,0:T(8,128)}) %reduce-scatter.2.cloned.1.call-update) | async-done | bytes 49168 | tf_op jit(solution)/shard_map/reduce_scatter | solution.py:80
  143.9 9.2 %psum.7 = f32[48,256]{1,0:T(8,128)S(1)} all-reduce(f32[48,256]{1,0:T(8,128)} %reduce-scatter.2.cloned.1.call-done), channel_id=1, replica_groups=mesh['dp'=2,'dom'=16] {'dp'}, use_global_device_ids=true, to_apply=%region_2.3 | all-reduce | flops 12288 | bytes 98304 | tf_op jit(solution)/shard_map/psum | solution.py:81
  153.1 21.6 %all_gather.3 = f32[768,256]{1,0:T(8,128)S(1)} all-gather(f32[48,256]{1,0:T(8,128)S(1)} %psum.7), channel_id=1, replica_groups=mesh['dp'=2,'dom'=16] {'dom'}, dimensions={0}, use_global_device_ids=true | all-gather | bytes 835584 | tf_op jit(solution)/shard_map/all_gather | solution.py:82
  174.7 0.8 slice_multiply_fusion
  175.5 0.7 slice_multiply_fusion.1
  (3 shorter events, 0.0 us)
Async XLA Ops:
  7.2 31.6 %copy-start = (bf16[8,4,128,128]{3,2,1,0:T(8,128)(2,1)S(1)}, bf16[8,4,128,128]{3,2,1,0:T(8,128)(2,1)}, u32[]{:S(2)}) copy-start(bf16[8,4,128,128]{3,2,1,0:T(8,128)(2,1)} %param.12) | copy-start | bytes 3145732
  14.5 8.5 %copy-start.9 = (s32[8]{0:T(128)S(1)}, s32[8]{0:T(128)}, u32[]{:S(2)}) copy-start(s32[8]{0:T(128)} %param.10) | copy-start | bytes 100
  14.5 22.9 %copy-start.7 = (bf16[256,256]{1,0:T(8,128)(2,1)S(1)}, bf16[256,256]{1,0:T(8,128)(2,1)}, u32[]{:S(2)}) copy-start(bf16[256,256]{1,0:T(8,128)(2,1)} %param.13) | copy-start | bytes 393220
  15.5 21.9 %all-to-all-start = ((bf16[16,64,256]{2,1,0:T(8,128)(2,1)}), bf16[16,64,256]{2,1,0:T(8,128)(2,1)S(1)}, u32[]{:S(2)}, u32[]{:S(2)}) async-start(bf16[16,64,256]{2,1,0:T(8,128)(2,1)} %broadcast_select_fusion), calls=%async_computation | async-start | bytes 1048576 | tf_op jit(solution)/shard_map/all_to_all | solution.py:28
  22.9 121.0 %reduce-scatter.2.cloned.1.call-start = ((), (), s32[]{:S(2)}) async-start(), calls=%async_computation.3 | async-start | bytes 835584 | tf_op jit(solution)/shard_map/reduce_scatter | solution.py:80
  37.4 28.3 %copy-start.2 = (bf16[16,64,256]{2,1,0:T(8,128)(2,1)}, bf16[16,64,256]{2,1,0:T(8,128)(2,1)S(1)}, u32[]{:S(2)}) copy-start(bf16[16,64,256]{2,1,0:T(8,128)(2,1)S(1)} %all-to-all-done) | copy-start | bytes 1572868
  41.5 5.5 %copy-start.8 = (s32[8,4]{0,1:T(4,128)S(1)}, s32[8,4]{0,1:T(4,128)}, u32[]{:S(2)}) copy-start(s32[8,4]{0,1:T(4,128)} %param.11) | copy-start | bytes 388
  51.3 14.4 %copy-start.5 = (bf16[1,1024,256]{2,1,0:T(8,128)(2,1)S(1)}, bf16[1,1024,256]{2,1,0:T(8,128)(2,1)}, u32[]{:S(2)}) copy-start(bf16[1,1024,256]{2,1,0:T(8,128)(2,1)} %param.15) | copy-start | bytes 1572868
  51.3 14.4 %copy-start.6 = (bf16[512,256]{1,0:T(8,128)(2,1)S(1)}, bf16[512,256]{1,0:T(8,128)(2,1)}, u32[]{:S(2)}) copy-start(bf16[512,256]{1,0:T(8,128)(2,1)} %param.14) | copy-start | bytes 786436
  51.3 9.4 %collective-permute-start = (bf16[8,128,256]{2,0,1:T(8,128)(2,1)S(1)}, bf16[8,128,256]{2,0,1:T(8,128)(2,1)S(1)}, u32[]{:S(2)}, u32[]{:S(2)}) collective-permute-start(bf16[8,128,256]{2,0,1:T(8,128)(2,1)S(1)} %get-tuple-element.4), channel_id=1, source_target_pairs={{0,15},{1,0},{2,1},{3,2},{4,3},{5,4},{6,5},{7,6},{8,7},{9,8},{10,9... | collective-permute-start | bytes 1572872 | tf_op jit(solution)/shard_map/ppermute | solution.py:11
  54.0 11.4 %collective-permute-start.1 = (bf16[8,128,256]{2,0,1:T(8,128)(2,1)S(1)}, bf16[8,128,256]{2,0,1:T(8,128)(2,1)S(1)}, u32[]{:S(2)}, u32[]{:S(2)}) collective-permute-start(bf16[8,128,256]{2,0,1:T(8,128)(2,1)S(1)} %get-tuple-element.5), channel_id=1, source_target_pairs={{0,1},{1,2},{2,3},{3,4},{4,5},{5,6},{6,7},{7,8},{8,9},{9,10},{10,1... | collective-permute-start | bytes 1572872 | tf_op jit(solution)/shard_map/ppermute | solution.py:11
  67.2 5.0 %copy-start.3 = (bf16[16,64,256]{2,1,0:T(8,128)(2,1)S(1)}, bf16[16,64,256]{2,1,0:T(8,128)(2,1)}, u32[]{:S(2)}) copy-start(bf16[16,64,256]{2,1,0:T(8,128)(2,1)} %copy-done.2) | copy-start | bytes 1572868
  67.8 11.5 %collective-permute-start.2 = (bf16[8,128,256]{2,1,0:T(8,128)(2,1)S(1)}, bf16[8,128,256]{2,1,0:T(8,128)(2,1)S(1)}, u32[]{:S(2)}, u32[]{:S(2)}) collective-permute-start(bf16[8,128,256]{2,1,0:T(8,128)(2,1)S(1)} %bitcast.71), channel_id=1, source_target_pairs={{0,1},{1,2},{2,3},{3,4},{4,5},{5,6},{6,7},{7,8},{8,9},{9,10},{10,1... | collective-permute-start | bytes 1572872 | tf_op jit(solution)/shard_map/ppermute | solution.py:11
  68.1 11.2 %collective-permute-start.3 = (bf16[8,128,256]{2,1,0:T(8,128)(2,1)S(1)}, bf16[8,128,256]{2,1,0:T(8,128)(2,1)S(1)}, u32[]{:S(2)}, u32[]{:S(2)}) collective-permute-start(bf16[8,128,256]{2,1,0:T(8,128)(2,1)S(1)} %bitcast.72), channel_id=1, source_target_pairs={{0,15},{1,0},{2,1},{3,2},{4,3},{5,4},{6,5},{7,6},{8,7},{9,8},{10,9... | collective-permute-start | bytes 1572872 | tf_op jit(solution)/shard_map/ppermute | solution.py:11
  80.7 1.2 copy-start.4
  82.3 0.8 copy-start.1
Sparse Core Ops, SparseCore 0:
  84.5 59.2 reduce-scatter.1
where the time goes:
time: 184 us; the launch traced here: 183 us
  waiting for transfers between devices  62.8 us (34%)
  blocking collectives  52.5 us (29%)
  local copies, waits for them, and re-layouts  17.8 us (10%)
  matrix products  14.8 us (8%)
  starting transfers between devices  14.6 us (8%)
  between operations  14.2 us (8%)
  other arithmetic  6.4 us (3%)
    reduce_scatter x1, waiting for transfers between devices, shards(): share = lax.psum_scatter(stacked, 'dom', scatter_dimension=0, tiled=True)  30.5 us
    all_to_all x1, blocking collectives, shards(): lax.all_to_all(d_nodes.reshape(ndom, per_peer, width), 'dom', split_axis=...  21.7 us
    all_gather x1, blocking collectives, shards(): whole = lax.all_gather(share, 'dom', axis=0, tiled=True)  21.6 us
    ppermute x4, waiting for transfers between devices, passed_along(): return lax.ppermute(x, axis, [(i, (i + by) % peers) for i in range(peers)])  17.9 us
    all_to_all x1, waiting for transfers between devices, shards(): lax.all_to_all(picked, 'dom', split_axis=0, concat_axis=0, tiled=True)  14.4 us
    psum x1, blocking collectives, shards(): share = lax.psum(share, 'dp')  9.2 us
    all_to_all x1, starting transfers between devices, shards(): lax.all_to_all(picked, 'dom', split_axis=0, concat_axis=0, tiled=True)  7.39 us
    ppermute x4, starting transfers between devices, passed_along(): return lax.ppermute(x, axis, [(i, (i + by) % peers) for i in range(peers)])  7.17 us
  transfers between devices with their start and end apart: 6, of which 5 were waited for; matrix products, arithmetic and copies ran while one was open for 4% of the time, Pallas kernels for 0%

commit v1 on v0

v1 whole, which is shorter than its diff:
```python
import functools
import math

import jax
import jax.numpy as jnp
from jax import lax
from jax.experimental import pallas as pl
from jax.experimental.pallas import tpu as pltpu
from jax.sharding import PartitionSpec as P

ROWS = 128
RIM = 2
VMEM = pl.BlockSpec(memory_space=pltpu.VMEM)
SMEM = pl.BlockSpec(memory_space=pltpu.SMEM)
BF16 = jnp.bfloat16
F32 = jnp.float32


def passed_along(x, axis, by):
    peers = lax.axis_size(axis)
    return lax.ppermute(x, axis, [(i, (i + by) % peers) for i in range(peers)])


def dsilu(value):
    sig = jax.nn.sigmoid(value)
    return sig * (1.0 + value * (1.0 - sig))


def dot(a, b, contract=((1,), (0,))):
    return lax.dot_general(a, b, (contract, ((), ())), preferred_element_type=F32)


def call(body, outs, args, specs, scratch=(), flops=0, nbytes=0):
    return pl.pallas_call(
        body,
        out_shape=outs,
        in_specs=specs,
        out_specs=[VMEM] * len(outs),
        scratch_shapes=list(scratch),
        cost_estimate=pl.CostEstimate(flops=flops, bytes_accessed=nbytes, transcendentals=0),
        compiler_params=pltpu.CompilerParams(vmem_limit_bytes=24 * 1024 * 1024),
    )(*args)


def pick_body(order_ref, feat_ref, out_ref):
    rows = feat_ref.shape[0]
    feat = feat_ref[...]
    lane = lax.broadcasted_iota(jnp.int32, (ROWS, rows), 1).astype(F32)
    for k in range(rows // ROWS):
        mine = slice(k * ROWS, (k + 1) * ROWS)
        row = order_ref[:, mine].astype(F32)
        col = jnp.transpose(jnp.broadcast_to(row, (ROWS, ROWS)))
        wide = jnp.concatenate([col] * (rows // ROWS), axis=1)
        hot = jnp.where(wide == lane, 1.0, 0.0).astype(BF16)
        out_ref[mine, :] = dot(hot, feat).astype(BF16)


def place_body(order_ref, back_ref, out_ref):
    rows = back_ref.shape[0]
    back = back_ref[...]
    order = jnp.broadcast_to(order_ref[...], (ROWS, rows))
    for k in range(rows // ROWS):
        mine = slice(k * ROWS, (k + 1) * ROWS)
        row = lax.broadcasted_iota(jnp.int32, (ROWS, rows), 0) + k * ROWS
        hot = jnp.where(order == row, 1.0, 0.0).astype(BF16)
        out_ref[mine, :] = dot(hot, back).astype(BF16)


def window_body(cnt_ref, tgt_ref, nodes_ref, vals_ref, w_edge_ref, prev_ref, own_ref, next_ref, win):
    blocks, slots = vals_ref.shape[0], vals_ref.shape[1]
    base = blocks - RIM
    trash = blocks + 2 * RIM
    win[...] = jnp.zeros_like(win)
    w_edge = w_edge_ref[...]
    for c in range(blocks):
        pre = dot(nodes_ref[c * ROWS : (c + 1) * ROWS, :], w_edge)
        message = (pre * jax.nn.sigmoid(pre)).astype(BF16)
        contrib = dot(vals_ref[c].reshape(slots * ROWS, ROWS), message)
        for s in range(slots):
            to = jnp.where(s < cnt_ref[c], tgt_ref[c, s] - base, trash)
            win[to] += contrib[s * ROWS : (s + 1) * ROWS, :]
    for b in range(RIM):
        prev_ref[b * ROWS : (b + 1) * ROWS, :] = win[b].astype(BF16)
        next_ref[b * ROWS : (b + 1) * ROWS, :] = win[RIM + blocks + b].astype(BF16)
    for b in range(blocks):
        own_ref[b * ROWS : (b + 1) * ROWS, :] = win[RIM + b].astype(BF16)


def node_body(
    nodes_ref, own_ref, from_prev_ref, from_next_ref, cot_ref, w_node_ref,
    out_ref, agg_ref, d_node_ref, d_nodes1_ref, d_agg_ref,
):
    rows, width = nodes_ref.shape
    w_node = w_node_ref[...]
    step = RIM * ROWS
    for k in range(rows // step):
        mine = slice(k * step, (k + 1) * step)
        agg = own_ref[mine, :].astype(F32)
        if k == 0:
            agg = agg + from_prev_ref[...].astype(F32)
        if k == rows // step - 1:
            agg = agg + from_next_ref[...].astype(F32)
        agg = agg.astype(BF16)
        agg_ref[mine, :] = agg
        nodes = nodes_ref[mine, :]
        pre = dot(nodes, w_node[:width]) + dot(agg, w_node[width:])
        sig = jax.nn.sigmoid(pre)
        out_ref[mine, :] = (nodes.astype(F32) + pre * sig).astype(BF16)
        gout = cot_ref[mine, :].astype(F32)
        d_node = (gout * (sig * (1.0 + pre * (1.0 - sig)))).astype(BF16)
        d_node_ref[mine, :] = d_node
        back = dot(d_node, w_node, ((1,), (1,)))
        d_nodes1_ref[mine, :] = gout + back[:, :width]
        d_agg_ref[mine, :] = back[:, width:].astype(BF16)


def grad_node_body(scale, nodes_ref, agg_ref, d_node_ref, out_ref):
    width = nodes_ref.shape[1]
    d_node = d_node_ref[...]
    out_ref[:width, :] = dot(nodes_ref[...], d_node, ((0,), (0,))) * scale
    out_ref[width:, :] = dot(agg_ref[...], d_node, ((0,), (0,))) * scale


def edge_body(
    cnt_ref, tgt_ref, nodes_ref, vals_ref, w_edge_ref, d_agg_ref, prev_ref, next_ref, d_nodes1_ref,
    d_nodes_ref, d_edge_ref, win,
):
    blocks, slots = vals_ref.shape[0], vals_ref.shape[1]
    base = blocks - RIM
    dead = blocks + 2 * RIM
    for b in range(RIM):
        win[b] = prev_ref[b * ROWS : (b + 1) * ROWS, :]
        win[RIM + blocks + b] = next_ref[b * ROWS : (b + 1) * ROWS, :]
    for b in range(blocks):
        win[RIM + b] = d_agg_ref[b * ROWS : (b + 1) * ROWS, :]
    win[dead] = jnp.zeros(win.shape[1:], BF16)
    w_edge = w_edge_ref[...]
    for c in range(blocks):
        mine = slice(c * ROWS, (c + 1) * ROWS)
        picked = []
        for s in range(slots):
            at = jnp.where(s < cnt_ref[c], tgt_ref[c, s] - base, dead)
            picked.append(win[at])
        picked = jnp.concatenate(picked, axis=0)
        d_message = dot(vals_ref[c].reshape(slots * ROWS, ROWS), picked, ((0,), (0,)))
        pre = dot(nodes_ref[mine, :], w_edge)
        d_edge = (d_message.astype(BF16).astype(F32) * dsilu(pre)).astype(BF16)
        d_edge_ref[mine, :] = d_edge
        d_nodes_ref[mine, :] = (d_nodes1_ref[mine, :] + dot(d_edge, w_edge, ((1,), (1,)))).astype(BF16)


def grad_edge_body(scale, nodes_ref, d_edge_ref, out_ref):
    out_ref[...] = dot(nodes_ref[...], d_edge_ref[...], ((0,), (0,))) * scale


def shards(features, send_order, adj_count, adj_target, adj_vals, w_edge, w_node, cotangent):
    ndom = lax.axis_size("dom")
    rows, width = features.shape[1:]
    per_peer = rows // ndom
    blocks, slots = adj_vals.shape[:2]
    rim = RIM * ROWS
    scale = 1.0 / math.sqrt(float(lax.axis_size("dp") * rows * ndom))
    tall = jax.ShapeDtypeStruct((rows, width), BF16)
    tall_f = jax.ShapeDtypeStruct((rows, width), F32)
    edge = jax.ShapeDtypeStruct((rim, width), BF16)
    unit = rows * width * 2

    (picked,) = call(
        pick_body, [tall], (send_order, features[0]), [VMEM, VMEM], flops=2 * rows * rows * width, nbytes=2 * unit
    )
    nodes = lax.all_to_all(
        picked.reshape(ndom, per_peer, width), "dom", split_axis=0, concat_axis=0, tiled=True
    ).reshape(rows, width)
    send_prev, own, send_next = call(
        window_body,
        [edge, tall, edge],
        (adj_count, adj_target, nodes, adj_vals, w_edge),
        [SMEM, SMEM, VMEM, VMEM, VMEM],
        [pltpu.VMEM((blocks + 2 * RIM + 1, ROWS, width), F32)],
        flops=2 * rows * width * (width + slots * ROWS),
        nbytes=4 * unit,
    )
    from_next = passed_along(send_prev, "dom", -1)
    from_prev = passed_along(send_next, "dom", 1)
    node_out, agg, d_node, d_nodes1, d_agg = call(
        node_body,
        [tall, tall, tall, tall_f, tall],
        (nodes, own, from_prev, from_next, cotangent[0], w_node),
        [VMEM] * 6,
        flops=8 * rows * width * width,
        nbytes=8 * unit,
    )
    prev_rows = passed_along(d_agg[rows - rim :], "dom", 1)
    next_rows = passed_along(d_agg[:rim], "dom", -1)
    (local_node,) = call(
        functools.partial(grad_node_body, scale),
        [jax.ShapeDtypeStruct((2 * width, width), F32)],
        (nodes, agg, d_node),
        [VMEM] * 3,
        flops=4 * rows * width * width,
        nbytes=3 * unit,
    )
    grad_node = lax.psum(local_node, ("dp", "dom"))
    d_nodes, d_edge = call(
        edge_body,
        [tall, tall],
        (adj_count, adj_target, nodes, adj_vals, w_edge, d_agg, prev_rows, next_rows, d_nodes1),
        [SMEM, SMEM] + [VMEM] * 7,
        [pltpu.VMEM((blocks + 2 * RIM + 1, ROWS, width), BF16)],
        flops=2 * rows * width * (2 * width + slots * ROWS),
        nbytes=6 * unit,
    )
    returned = lax.all_to_all(
        d_nodes.reshape(ndom, per_peer, width), "dom", split_axis=0, concat_axis=0, tiled=True
    ).reshape(rows, width)
    (local_edge,) = call(
        functools.partial(grad_edge_body, scale),
        [jax.ShapeDtypeStruct((width, width), F32)],
        (nodes, d_edge),
        [VMEM] * 2,
        flops=2 * rows * width * width,
        nbytes=2 * unit,
    )
    grad_edge = lax.psum(local_edge, ("dp", "dom"))
    (grad_brick,) = call(
        place_body, [tall], (send_order, returned), [VMEM, VMEM], flops=2 * rows * rows * width, nbytes=2 * unit
    )
    return (node_out[None], grad_brick[None], grad_edge, grad_node)


def solution(mesh):
    in_specs = (
        P("dp", "dom", None),
        P("dom", None),
        P("dom"),
        P("dom", None),
        P("dom", None, None, None),
        P(),
        P(),
        P("dp", "dom", None),
    )
    out_specs = (P("dp", "dom", None), P("dp", "dom", None), P(), P())
    return jax.shard_map(shards, mesh=mesh, in_specs=in_specs, out_specs=out_specs, check_vma=False)
```

time: 184 us -> 207 us (1.12)
  waiting for transfers between devices: 62.8 us -> 153 us
  blocking collectives: 52.5 us -> 0 us
  matrix products: 14.8 us -> 0 us
  local copies, waits for them, and re-layouts: 17.8 us -> 4.38 us
  Pallas kernels: 0 us -> 12.3 us
  starting transfers between devices: 14.6 us -> 22.5 us
  other arithmetic: 6.4 us -> 0 us
    psum x0 -> x1, waiting for transfers between devices: none -> 122 us  [shards(): grad_edge = lax.psum(local_edge, ('dp', 'dom'))]
    reduce_scatter x1 -> x0, waiting for transfers between devices: 30.5 us -> none  [shards(): share = lax.psum_scatter(stacked, 'dom', scatter_dimension=0, tiled=True)]
    all_to_all x1 -> x0, blocking collectives: 21.7 us -> none  [shards(): lax.all_to_all(d_nodes.reshape(ndom, per_peer, width), 'dom', split_axis=...]
    all_gather x1 -> x0, blocking collectives: 21.6 us -> none  [shards(): whole = lax.all_gather(share, 'dom', axis=0, tiled=True)]
    dot_general x10 -> x0, matrix products: 14.8 us -> none  [the longest x1 4.16 us: shards(): jnp.einsum('wcs,csrh->wrh', table_f, contrib, precision=lax.Precision.HIG...]
    ppermute x4, waiting for transfers between devices: 17.9 us -> 5.24 us  [passed_along(): return lax.ppermute(x, axis, [(i, (i + by) % peers) for i in range(peers)])]
    pallas_call x0 -> x7, Pallas kernels: none -> 12.3 us  [call(): pl.pallas_call(body, out_shape=outs, in_specs=specs, out_specs=[VMEM] * l...]
    all_to_all x1 -> x2, waiting for transfers between devices: 14.4 us -> 26.4 us  [the longest x1 14.4 us: shards(): lax.all_to_all(picked.reshape(ndom, per_peer, width), 'dom', split_axis=0...]
  transfers between devices with their start and end apart: 6 -> 7, of which waited for: 5 -> 5; matrix products, arithmetic and copies ran while one was open for 4% -> 0% of each run, Pallas kernels for 0% -> 2%
where the time goes in v1:
time: 207 us
  waiting for transfers between devices  153 us (74%)
  starting transfers between devices  22.5 us (11%)
  between operations  14.1 us (7%)
  Pallas kernels  12.3 us (6%)
  local copies, waits for them, and re-layouts  4.38 us (2%)
    psum x1, waiting for transfers between devices, shards(): grad_edge = lax.psum(local_edge, ('dp', 'dom'))  122 us
    all_to_all x1, waiting for transfers between devices, shards(): lax.all_to_all(picked.reshape(ndom, per_peer, width), 'dom', split_axis=0...  14.4 us
    pallas_call x7, Pallas kernels, call(): pl.pallas_call(body, out_shape=outs, in_specs=specs, out_specs=[VMEM] * l...  12.3 us
    all_to_all x1, waiting for transfers between devices, shards(): lax.all_to_all(d_nodes.reshape(ndom, per_peer, width), 'dom', split_axis=...  12 us
    ppermute x4, starting transfers between devices, passed_along(): return lax.ppermute(x, axis, [(i, (i + by) % peers) for i in range(peers)])  9.05 us
    all_to_all x1, starting transfers between devices, shards(): lax.all_to_all(picked.reshape(ndom, per_peer, width), 'dom', split_axis=0...  7.52 us
    all_to_all x1, starting transfers between devices, shards(): lax.all_to_all(d_nodes.reshape(ndom, per_peer, width), 'dom', split_axis=...  5.88 us
    ppermute x4, waiting for transfers between devices, passed_along(): return lax.ppermute(x, axis, [(i, (i + by) % peers) for i in range(peers)])  5.24 us
  transfers between devices with their start and end apart: 7, of which 5 were waited for; matrix products, arithmetic and copies ran while one was open for 0% of the time, Pallas kernels for 2%

profile of v1, /device:TPU:0, one launch (start us, length us, event | category | flops | bytes accessed | tf_op | source)
XLA Modules:
  0.0 206.6 jit_solution(15040780079376993715)
XLA Ops:
  7.2 0.0 copy-start.5
  7.2 1.0 copy-done.5
  8.2 0.0 copy-start.6
  8.2 0.7 copy-done.6
  8.9 0.0 copy-start
  8.9 1.6 shard_map.111
  10.5 0.0 copy-start.9
  10.5 0.0 copy-start.1
  10.5 7.5 %all-to-all-start = ((bf16[16,64,256]{2,1,0:T(8,128)(2,1)}), bf16[16,64,256]{2,1,0:T(8,128)(2,1)S(1)}, u32[]{:S(2)}, u32[]{:S(2)}) async-start(bf16[16,64,256]{2,1,0:T(8,128)(2,1)} %bitcast.1), calls=%async_computation | async-start | bytes 1048576 | tf_op jit(solution)/shard_map/all_to_all | solution.py:171
  18.0 0.0 copy-done.9
  18.0 0.1 copy.12.tgt_ref
  18.1 0.0 copy-start.4
  18.1 14.4 %all-to-all-done = bf16[16,64,256]{2,1,0:T(8,128)(2,1)S(1)} async-done(((bf16[16,64,256]{2,1,0:T(8,128)(2,1)}), bf16[16,64,256]{2,1,0:T(8,128)(2,1)S(1)}, u32[]{:S(2)}, u32[]{:S(2)}) %all-to-all-start) | async-done | bytes 524320 | tf_op jit(solution)/shard_map/all_to_all | solution.py:171
  32.5 0.0 copy-done
  32.5 0.0 copy-done.1
  32.5 0.0 copy-done.4
  32.5 0.0 copy-start.2
  32.5 0.0 copy-start.3
  32.5 2.2 %shard_map.112 = (bf16[256,256]{1,0:T(8,128)(2,1)S(1)}, bf16[1024,256]{1,0:T(8,128)(2,1)S(1)}, bf16[256,256]{1,0:T(8,128)(2,1)S(1)}) custom-call(s32[8]{0:T(128)S(1)} %copy-done.4, s32[8,4]{1,0:T(8,128)S(1)} %copy.12.tgt_ref, bf16[1024,256]{1,0:T(8,128)(2,1)S(1)} %bitcast.8, bf16[8,4,128,128]{3,2,1,0:T(8,128)(2,1)S(1)} %copy-done, bf16[256,256]{1,0:T(8,128)(2,1)S(1)} %copy-done.1), custom_call_target="tpu_custom_call" | custom-call | flops 402653184 | bytes 2097152 | tf_op jit(solution)/shard_map/pallas_call | solution.py:34
  34.7 0.1 collective-permute-start
  34.8 4.4 %collective-permute-start.1 = (bf16[256,256]{1,0:T(8,128)(2,1)S(1)}, bf16[256,256]{1,0:T(8,128)(2,1)S(1)}, u32[]{:S(2)}, u32[]{:S(2)}) collective-permute-start(bf16[256,256]{1,0:T(8,128)(2,1)S(1)} %get-tuple-element.16), channel_id=1, source_target_pairs={{0,15},{1,0},{2,1},{3,2},{4,3},{5,4},{6,5},{7,6},{8,7},{9,8},{10,9... | collective-permute-start | bytes 393224 | tf_op jit(solution)/shard_map/ppermute | solution.py:21
  39.2 2.6 %collective-permute-done.from_prev_ref = bf16[256,256]{1,0:T(8,128)(2,1)S(1)} collective-permute-done((bf16[256,256]{1,0:T(8,128)(2,1)S(1)}, bf16[256,256]{1,0:T(8,128)(2,1)S(1)}, u32[]{:S(2)}, u32[]{:S(2)}) %collective-permute-start) | collective-permute-done | bytes 131104 | tf_op jit(solution)/shard_map/ppermute | solution.py:21
  41.8 0.0 collective-permute-done.1.from_next_ref
  41.8 0.0 copy-done.2
  41.8 0.0 copy-done.3
  41.9 1.7 shard_map.113
  43.6 0.1 collective-permute-start.2
  43.6 4.5 %collective-permute-start.3 = (bf16[256,256]{1,0:T(8,128)(2,1)S(1)}, bf16[256,256]{1,0:T(8,128)(2,1)S(1)}, u32[]{:S(2)}, u32[]{:S(2)}) collective-permute-start(bf16[256,256]{1,0:T(8,128)(2,1)S(1)} %get-tuple-element.26), channel_id=1, source_target_pairs={{0,15},{1,0},{2,1},{3,2},{4,3},{5,4},{6,5},{7,6},{8,7},{9,8},{10,9... | collective-permute-start | bytes 393224 | tf_op jit(solution)/shard_map/ppermute | solution.py:21
  48.1 2.6 %collective-permute-done.2.prev_ref = bf16[256,256]{1,0:T(8,128)(2,1)S(1)} collective-permute-done((bf16[256,256]{1,0:T(8,128)(2,1)S(1)}, bf16[256,256]{1,0:T(8,128)(2,1)S(1)}, u32[]{:S(2)}, u32[]{:S(2)}) %collective-permute-start.2) | collective-permute-done | bytes 131104 | tf_op jit(solution)/shard_map/ppermute | solution.py:21
  50.7 0.0 collective-permute-done.3.next_ref
  50.7 3.0 %shard_map.114 = (bf16[1024,256]{1,0:T(8,128)(2,1)}, bf16[1024,256]{1,0:T(8,128)(2,1)S(1)}) custom-call(s32[8]{0:T(128)S(1)} %copy-done.4, s32[8,4]{1,0:T(8,128)S(1)} %copy.12.tgt_ref, bf16[1024,256]{1,0:T(8,128)(2,1)S(1)} %bitcast.10, bf16[8,4,128,128]{3,2,1,0:T(8,128)(2,1)S(1)} %copy-done, bf16[256,256]{1,0:T(8,128)(2,1)S(1)} %copy-done.1, ...), custom_call_target="tpu_custom_call" | custom-call | flops 536870912 | bytes 3145728 | tf_op jit(solution)/shard_map/pallas_call | solution.py:34
  53.7 5.9 %all-to-all-start.1 = ((bf16[16,64,256]{2,1,0:T(8,128)(2,1)}), bf16[16,64,256]{2,1,0:T(8,128)(2,1)S(1)}, u32[]{:S(2)}, u32[]{:S(2)}) async-start(bf16[16,64,256]{2,1,0:T(8,128)(2,1)} %bitcast.5), calls=%async_computation.1 | async-start | bytes 1048576 | tf_op jit(solution)/shard_map/all_to_all | solution.py:213
  59.6 0.0 all-reduce.3.cloned.1.call-start
  59.7 1.3 shard_map.117
  60.9 1.1 shard_map.116
  62.0 0.0 copy-start.7
  62.0 0.0 all-reduce.3.cloned.1.call-update
  62.0 12.0 %all-to-all-done.1 = bf16[16,64,256]{2,1,0:T(8,128)(2,1)S(1)} async-done(((bf16[16,64,256]{2,1,0:T(8,128)(2,1)}), bf16[16,64,256]{2,1,0:T(8,128)(2,1)S(1)}, u32[]{:S(2)}, u32[]{:S(2)}) %all-to-all-start.1) | async-done | bytes 524320 | tf_op jit(solution)/shard_map/all_to_all | solution.py:213
  74.1 0.0 copy-done.7
  74.1 1.5 shard_map.115
  75.6 121.6 %all-reduce.3.cloned.1.call-done = (f32[256,256]{1,0:T(8,128)}, f32[512,256]{1,0:T(8,128)}) async-done(((f32[256,256]{1,0:T(8,128)}, f32[512,256]{1,0:T(8,128)}), (f32[256,256]{1,0:T(8,128)}, f32[512,256]{1,0:T(8,128)})) %all-reduce.3.cloned.1.call-update) | async-done | bytes 786448 | tf_op jit(solution)/shard_map/psum | solution.py:224
  197.2 0.0 copy-start.8
  197.2 1.7 copy.16
  198.9 0.0 copy-done.8
  198.9 0.8 copy.17
  (1 shorter events, 0.0 us)
Async XLA Ops:
  7.2 1.0 copy-start.5
  8.2 0.7 copy-start.6
  8.9 23.6 %copy-start = (bf16[8,4,128,128]{3,2,1,0:T(8,128)(2,1)S(1)}, bf16[8,4,128,128]{3,2,1,0:T(8,128)(2,1)}, u32[]{:S(2)}) copy-start(bf16[8,4,128,128]{3,2,1,0:T(8,128)(2,1)} %vals_ref.3) | copy-start | bytes 3145732
  10.5 7.5 %copy-start.9 = (s32[8,4]{0,1:T(4,128)S(1)}, s32[8,4]{0,1:T(4,128)}, u32[]{:S(2)}) copy-start(s32[8,4]{0,1:T(4,128)} %param.11) | copy-start | bytes 388
  10.5 22.0 %copy-start.1 = (bf16[256,256]{1,0:T(8,128)(2,1)S(1)}, bf16[256,256]{1,0:T(8,128)(2,1)}, u32[]{:S(2)}) copy-start(bf16[256,256]{1,0:T(8,128)(2,1)} %w_edge_ref.3) | copy-start | bytes 393220
  10.5 22.0 %all-to-all-start = ((bf16[16,64,256]{2,1,0:T(8,128)(2,1)}), bf16[16,64,256]{2,1,0:T(8,128)(2,1)S(1)}, u32[]{:S(2)}, u32[]{:S(2)}) async-start(bf16[16,64,256]{2,1,0:T(8,128)(2,1)} %bitcast.1), calls=%async_computation | async-start | bytes 1048576 | tf_op jit(solution)/shard_map/all_to_all | solution.py:171
  18.1 14.4 %copy-start.4 = (s32[8]{0:T(128)S(1)}, s32[8]{0:T(128)}, u32[]{:S(2)}) copy-start(s32[8]{0:T(128)} %cnt_ref.3) | copy-start | bytes 100
  32.5 9.4 %copy-start.2 = (bf16[1,1024,256]{2,1,0:T(8,128)(2,1)S(1)}, bf16[1,1024,256]{2,1,0:T(8,128)(2,1)}, u32[]{:S(2)}) copy-start(bf16[1,1024,256]{2,1,0:T(8,128)(2,1)} %param.15) | copy-start | bytes 1572868
  32.5 9.4 %copy-start.3 = (bf16[512,256]{1,0:T(8,128)(2,1)S(1)}, bf16[512,256]{1,0:T(8,128)(2,1)}, u32[]{:S(2)}) copy-start(bf16[512,256]{1,0:T(8,128)(2,1)} %w_node_ref.1) | copy-start | bytes 786436
  34.7 7.1 %collective-permute-start = (bf16[256,256]{1,0:T(8,128)(2,1)S(1)}, bf16[256,256]{1,0:T(8,128)(2,1)S(1)}, u32[]{:S(2)}, u32[]{:S(2)}) collective-permute-start(bf16[256,256]{1,0:T(8,128)(2,1)S(1)} %get-tuple-element.15), channel_id=1, source_target_pairs={{0,1},{1,2},{2,3},{3,4},{4,5},{5,6},{6,7},{7,8},{8,9},{9,10},{10,1... | collective-permute-start | bytes 393224 | tf_op jit(solution)/shard_map/ppermute | solution.py:21
  34.8 7.1 %collective-permute-start.1 = (bf16[256,256]{1,0:T(8,128)(2,1)S(1)}, bf16[256,256]{1,0:T(8,128)(2,1)S(1)}, u32[]{:S(2)}, u32[]{:S(2)}) collective-permute-start(bf16[256,256]{1,0:T(8,128)(2,1)S(1)} %get-tuple-element.16), channel_id=1, source_target_pairs={{0,15},{1,0},{2,1},{3,2},{4,3},{5,4},{6,5},{7,6},{8,7},{9,8},{10,9... | collective-permute-start | bytes 393224 | tf_op jit(solution)/shard_map/ppermute | solution.py:21
  43.6 7.2 %collective-permute-start.2 = (bf16[256,256]{1,0:T(8,128)(2,1)S(1)}, bf16[256,256]{1,0:T(8,128)(2,1)S(1)}, u32[]{:S(2)}, u32[]{:S(2)}) collective-permute-start(bf16[256,256]{1,0:T(8,128)(2,1)S(1)} %get-tuple-element.27), channel_id=1, source_target_pairs={{0,1},{1,2},{2,3},{3,4},{4,5},{5,6},{6,7},{7,8},{8,9},{9,10},{10,1... | collective-permute-start | bytes 393224 | tf_op jit(solution)/shard_map/ppermute | solution.py:21
  43.6 7.1 %collective-permute-start.3 = (bf16[256,256]{1,0:T(8,128)(2,1)S(1)}, bf16[256,256]{1,0:T(8,128)(2,1)S(1)}, u32[]{:S(2)}, u32[]{:S(2)}) collective-permute-start(bf16[256,256]{1,0:T(8,128)(2,1)S(1)} %get-tuple-element.26), channel_id=1, source_target_pairs={{0,15},{1,0},{2,1},{3,2},{4,3},{5,4},{6,5},{7,6},{8,7},{9,8},{10,9... | collective-permute-start | bytes 393224 | tf_op jit(solution)/shard_map/ppermute | solution.py:21
  53.7 20.4 %all-to-all-start.1 = ((bf16[16,64,256]{2,1,0:T(8,128)(2,1)}), bf16[16,64,256]{2,1,0:T(8,128)(2,1)S(1)}, u32[]{:S(2)}, u32[]{:S(2)}) async-start(bf16[16,64,256]{2,1,0:T(8,128)(2,1)} %bitcast.5), calls=%async_computation.1 | async-start | bytes 1048576 | tf_op jit(solution)/shard_map/all_to_all | solution.py:213
  59.6 137.6 %all-reduce.3.cloned.1.call-start = ((), (), s32[]{:S(2)}) async-start(), calls=%async_computation.2 | async-start | bytes 1572864 | tf_op jit(solution)/shard_map/psum | solution.py:224
  62.0 12.1 %copy-start.7 = (s32[1,1024]{1,0:T(1,128)S(1)}, s32[1,1024]{1,0:T(1,128)}, u32[]{:S(2)}) copy-start(s32[1,1024]{1,0:T(1,128)} %order_ref.3) | copy-start | bytes 12292
  197.2 1.7 copy-start.8
Sparse Core Ops, SparseCore 0:
  66.4 130.7 all-reduce.2

commit v2 on v0

v2 whole, which is shorter than its diff:
```python
import functools
import math

import jax
import jax.numpy as jnp
from jax import lax
from jax.experimental import pallas as pl
from jax.experimental.pallas import tpu as pltpu
from jax.sharding import PartitionSpec as P

ROWS = 128
RIM = 2
ANY = pl.BlockSpec(memory_space=pl.ANY)
VMEM = pl.BlockSpec(memory_space=pltpu.VMEM)
SMEM = pl.BlockSpec(memory_space=pltpu.SMEM)
BF16 = jnp.bfloat16
F32 = jnp.float32
MIB = 1024 * 1024


def swapped(x, axis, mask):
    peers = lax.axis_size(axis)
    return lax.ppermute(x, axis, [(i, i ^ mask) for i in range(peers)])


def swapped_across(x, axis):
    peers = lax.axis_size(axis)
    return lax.ppermute(x, axis, [(i, (i + 1 if i % 2 else i - 1) % peers) for i in range(peers)])


def dot(a, b, contract=((1,), (0,))):
    return lax.dot_general(a, b, (contract, ((), ())), preferred_element_type=F32)


def shape(*dims, dtype=BF16):
    return jax.ShapeDtypeStruct(dims, dtype)


def call(body, outs, args, specs=None, scratch=(), flops=0, nbytes=0, limit=24 * MIB):
    return pl.pallas_call(
        body,
        out_shape=outs,
        in_specs=specs or [VMEM] * len(args),
        out_specs=[VMEM] * len(outs),
        scratch_shapes=list(scratch),
        cost_estimate=pl.CostEstimate(flops=flops, bytes_accessed=nbytes, transcendentals=0),
        compiler_params=pltpu.CompilerParams(vmem_limit_bytes=limit),
    )(*args)


def pick_body(order_hbm, feat_hbm, out_ref, order_ref, feat_ref, order_sem, feat_sem):
    rows = feat_ref.shape[0]
    load_order = pltpu.make_async_copy(order_hbm, order_ref, order_sem)
    load_feat = pltpu.make_async_copy(feat_hbm, feat_ref, feat_sem)
    load_order.start()
    load_feat.start()
    load_order.wait()
    load_feat.wait()
    feat = feat_ref[...]
    lane = lax.broadcasted_iota(jnp.int32, (ROWS, rows), 1).astype(F32)
    for k in range(rows // ROWS):
        mine = slice(k * ROWS, (k + 1) * ROWS)
        row = order_ref[:, mine].astype(F32)
        col = jnp.transpose(jnp.broadcast_to(row, (ROWS, ROWS)))
        wide = jnp.concatenate([col] * (rows // ROWS), axis=1)
        hot = jnp.where(wide == lane, 1.0, 0.0).astype(BF16)
        out_ref[mine, :] = dot(hot, feat).astype(BF16)


def build_body(cnt_ref, tgt_ref, vals_ref, a_ref, at_ref):
    blocks, slots = vals_ref.shape[:2]
    spare = blocks + 2 * RIM
    a_ref[...] = jnp.zeros_like(a_ref)
    at_ref[...] = jnp.zeros_like(at_ref)
    for c in range(blocks):
        mine = slice(c * ROWS, (c + 1) * ROWS)
        for s in range(slots):
            w = tgt_ref[c, s]
            at = jnp.where(w < blocks, w + RIM, jnp.where(w < 2 * blocks, w - blocks, w - blocks + RIM))
            at = jnp.where(s < cnt_ref[c], at, spare)
            value = vals_ref[c, s].astype(F32)
            a_ref[at, :, mine] = (a_ref[at, :, mine].astype(F32) + value).astype(BF16)
            lanes = pl.ds(pl.multiple_of(at * ROWS, ROWS), ROWS)
            at_ref[mine, lanes] = (at_ref[mine, lanes].astype(F32) + jnp.transpose(value)).astype(BF16)


def chosen(first, second):
    odd = lax.rem(lax.axis_index("dom"), 2) == 1
    return jnp.where(odd, first, second), jnp.where(odd, second, first)


def message_body(nodes_ref, a_ref, w_edge_ref, near_ref, far_ref, msg_ref):
    rows = nodes_ref.shape[0]
    rim = RIM * ROWS
    for k in range(rows // rim):
        mine = slice(k * rim, (k + 1) * rim)
        pre = dot(nodes_ref[mine, :], w_edge_ref[...])
        msg_ref[mine, :] = (pre * jax.nn.sigmoid(pre)).astype(BF16)
    blocks = rows // ROWS
    sums = dot(a_ref[blocks : blocks + 2 * RIM].reshape(2 * rim, rows), msg_ref[...])
    near, far = chosen(sums[:rim], sums[rim:])
    near_ref[...] = near.astype(BF16)
    far_ref[...] = far.astype(BF16)


def node_step(nodes, agg, gout, w_node):
    width = nodes.shape[1]
    pre = dot(nodes, w_node[:width]) + dot(agg, w_node[width:])
    sig = jax.nn.sigmoid(pre)
    out = (nodes.astype(F32) + pre * sig).astype(BF16)
    gout = gout.astype(F32)
    d_node = (gout * (sig * (1.0 + pre * (1.0 - sig)))).astype(BF16)
    back = dot(d_node, w_node, ((1,), (1,)))
    return out, d_node, gout + back[:, :width], back[:, width:].astype(BF16)


def own_body(
    nodes_ref, msg_ref, a_ref, cot_ref, w_node_ref,
    own_ref, out_ref, agg_ref, d_node_ref, d_nodes1_ref, d_agg_ref,
):
    rows, width = nodes_ref.shape
    rim = RIM * ROWS
    msg = msg_ref[...]
    for k in range(rows // rim):
        mine = slice(k * rim, (k + 1) * rim)
        window = dot(a_ref[k * RIM : (k + 1) * RIM].reshape(rim, rows), msg).astype(BF16)
        if k == 0:
            own_ref[:rim, :] = window
        elif k == rows // rim - 1:
            own_ref[rim:, :] = window
        else:
            here = slice((k - 1) * rim, k * rim)
            agg_ref[here, :] = window
            out, d_node, d_nodes1, d_agg = node_step(nodes_ref[mine, :], window, cot_ref[mine, :], w_node_ref[...])
            out_ref[here, :] = out
            d_node_ref[here, :] = d_node
            d_nodes1_ref[here, :] = d_nodes1
            d_agg_ref[here, :] = d_agg


def rim_body(
    nodes_ref, own_ref, near_in_ref, far_in_ref, cot_ref, w_node_ref,
    near_ref, far_ref, out_ref, agg_ref, d_node_ref, d_nodes1_ref, d_agg_ref,
):
    rows = nodes_ref.shape[0]
    rim = RIM * ROWS
    arrived = chosen(near_in_ref[...].astype(F32), far_in_ref[...].astype(F32))
    rims = []
    for k in range(2):
        mine = slice(k * (rows - rim), k * (rows - rim) + rim)
        here = slice(k * rim, (k + 1) * rim)
        agg = (own_ref[here, :].astype(F32) + arrived[k]).astype(BF16)
        agg_ref[here, :] = agg
        out, d_node, d_nodes1, d_agg = node_step(nodes_ref[mine, :], agg, cot_ref[mine, :], w_node_ref[...])
        out_ref[here, :] = out
        d_node_ref[here, :] = d_node
        d_nodes1_ref[here, :] = d_nodes1
        d_agg_ref[here, :] = d_agg
        rims.append(d_agg)
    near_ref[...], far_ref[...] = chosen(rims[0], rims[1])


def in_order(mid_ref, rim_ref):
    rim = RIM * ROWS
    return jnp.concatenate([rim_ref[:rim, :], mid_ref[...], rim_ref[rim:, :]], axis=0)


def grad_node_body(scale, nodes_ref, agg_mid_ref, agg_rim_ref, d_node_mid_ref, d_node_rim_ref, *out_refs):
    width = nodes_ref.shape[1]
    d_node = in_order(d_node_mid_ref, d_node_rim_ref)
    agg = in_order(agg_mid_ref, agg_rim_ref)
    first = lax.axis_index("dp") == 0
    for k, left in enumerate((nodes_ref[...], agg)):
        mine = slice(k * width, (k + 1) * width)
        grad = dot(left, d_node, ((0,), (0,))) * scale
        if len(out_refs) == 1:
            out_refs[0][mine, :] = grad.astype(BF16)
            continue
        half = width // 2
        out_refs[0][mine, :] = jnp.where(first, grad[:, :half], grad[:, half:])
        out_refs[1][mine, :] = jnp.where(first, grad[:, half:], grad[:, :half]).astype(BF16)


def behind_body(
    nodes_ref, at_ref, w_edge_ref, out_mid_ref, out_rim_ref, d_agg_mid_ref, d_agg_rim_ref,
    out_ref, d_msg_ref, slope_ref,
):
    rows = nodes_ref.shape[0]
    rim = RIM * ROWS
    out_ref[...] = in_order(out_mid_ref, out_rim_ref)
    d_agg = in_order(d_agg_mid_ref, d_agg_rim_ref)
    for k in range(rows // rim):
        mine = slice(k * rim, (k + 1) * rim)
        d_msg_ref[mine, :] = dot(at_ref[mine, :rows], d_agg)
        pre = dot(nodes_ref[mine, :], w_edge_ref[...])
        sig = jax.nn.sigmoid(pre)
        slope_ref[mine, :] = sig * (1.0 + pre * (1.0 - sig))


def edge_body(
    scale, tiled, nodes_ref, at_ref, near_ref, far_ref, d_msg_ref, slope_ref, mid_ref, rim_ref, w_edge_ref, *refs
):
    back_ref, d_edge_ref = refs[-2 if tiled else -3], refs[-1]
    rows, width = nodes_ref.shape
    rim = RIM * ROWS
    peers = back_ref.shape[0]
    per_peer = rows // peers
    prev, after = chosen(near_ref[...], far_ref[...])
    rims = jnp.concatenate([prev, after], axis=0)
    w_edge = w_edge_ref[...]
    for k in range(rows // rim):
        mine = slice(k * rim, (k + 1) * rim)
        d_msg = d_msg_ref[mine, :] + dot(at_ref[mine, rows : rows + 2 * rim], rims)
        d_edge = (d_msg.astype(BF16).astype(F32) * slope_ref[mine, :]).astype(BF16)
        d_edge_ref[mine, :] = d_edge
        if k == 0:
            d_nodes1 = rim_ref[:rim, :]
        elif k == rows // rim - 1:
            d_nodes1 = rim_ref[rim:, :]
        else:
            d_nodes1 = mid_ref[(k - 1) * rim : k * rim, :]
        d_nodes = (d_nodes1 + dot(d_edge, w_edge, ((1,), (1,)))).astype(BF16)
        for p in range(rim // per_peer):
            back_ref[k * (rim // per_peer) + p, :per_peer, :] = d_nodes[p * per_peer : (p + 1) * per_peer, :]
    g_edge = (dot(nodes_ref[...], d_edge_ref[...], ((0,), (0,))) * scale).astype(BF16)
    if not tiled:
        refs[-2][...] = g_edge
        return
    keep_ref, recv_ref = refs[:2]
    g_node = (keep_ref[...] + recv_ref[...].astype(F32)).astype(BF16)
    share = width // peers
    half = width // 2
    for p in range(peers):
        back_ref[p, per_peer : per_peer + share, :] = g_edge[p * share : (p + 1) * share, :]
        row = 2 * p * share
        back_ref[p, per_peer + share :, :half] = g_node[row : row + share, :]
        back_ref[p, per_peer + share :, half:] = g_node[row + share : row + 2 * share, :]


def share_body(back_ref, out_ref):
    share = out_ref.shape[1]
    total = jnp.sum(back_ref[:, back_ref.shape[1] - share :, :].astype(F32), axis=0).astype(BF16)
    out_ref[...] = jnp.broadcast_to(total[None], out_ref.shape)


def finish_body(parts_ref, edge_ref, node_ref):
    share = parts_ref.shape[1] // 2
    half = parts_ref.shape[2] // 2
    peers = parts_ref.shape[0] // 2
    for p in range(peers):
        one, two = parts_ref[p].astype(F32), parts_ref[peers + p].astype(F32)
        edge_ref[p * share : (p + 1) * share, :] = one[:share] + two[:share]
        row = 2 * p * share
        for k, part in enumerate((one[share:], two[share:])):
            lanes = slice(k * half, (k + 1) * half)
            node_ref[row : row + share, lanes] = part[:, :half]
            node_ref[row + share : row + 2 * share, lanes] = part[:, half:]


def place_body(order_ref, back_ref, out_ref):
    rows, width = out_ref.shape
    per_peer = rows // back_ref.shape[0]
    back = back_ref[:, :per_peer, :].reshape(rows, width)
    order = jnp.broadcast_to(order_ref[...], (ROWS, rows))
    for k in range(rows // ROWS):
        mine = slice(k * ROWS, (k + 1) * ROWS)
        row = lax.broadcasted_iota(jnp.int32, (ROWS, rows), 0) + k * ROWS
        hot = jnp.where(order == row, 1.0, 0.0).astype(BF16)
        out_ref[mine, :] = dot(hot, back).astype(BF16)


def shards(features, send_order, adj_count, adj_target, adj_vals, w_edge, w_node, cotangent):
    ndp = lax.axis_size("dp")
    ndom = lax.axis_size("dom")
    rows, width = features.shape[1:]
    per_peer = rows // ndom
    blocks, slots = adj_vals.shape[:2]
    rim = RIM * ROWS
    scale = 1.0 / math.sqrt(float(ndp * rows * ndom))
    tall = shape(rows, width)
    tall_f = shape(rows, width, dtype=F32)
    edge = shape(rim, width)
    rims = shape(2 * rim, width)
    mid = shape(rows - 2 * rim, width)
    unit = rows * width * 2
    square = 2 * rows * width * width
    share = width // ndom
    tiled = ndp == 2 and share % 16 == 0

    (picked,) = call(
        pick_body,
        [tall],
        (send_order, features[0]),
        [ANY, ANY],
        [
            pltpu.VMEM((1, rows), jnp.int32),
            pltpu.VMEM((rows, width), BF16),
            pltpu.SemaphoreType.DMA,
            pltpu.SemaphoreType.DMA,
        ],
        flops=2 * rows * rows * width,
        nbytes=2 * unit,
        limit=56 * MIB,
    )
    nodes = lax.all_to_all(
        picked.reshape(ndom, per_peer, width), "dom", split_axis=0, concat_axis=0, tiled=True
    ).reshape(rows, width)
    spots = blocks + 2 * RIM + 1
    adj, adj_t = call(
        build_body,
        [shape(spots, ROWS, rows), shape(rows, spots * ROWS)],
        (adj_count, adj_target, adj_vals),
        [SMEM, SMEM, VMEM],
        nbytes=16 * unit,
    )
    near, far, msg = call(
        message_body, [edge, edge, tall], (nodes, adj, w_edge), flops=square + 4 * rim * rows * width, nbytes=4 * unit
    )
    far = swapped_across(far, "dom")
    near = swapped(near, "dom", 1)
    cot = cotangent[0]
    own, out_mid, agg_mid, d_node_mid, d_nodes1_mid, d_agg_mid = call(
        own_body,
        [rims, mid, mid, mid, shape(*mid.shape, dtype=F32), mid],
        (nodes, msg, adj, cot, w_node),
        flops=2 * rows * rows * width + 2 * square,
        nbytes=8 * unit,
    )
    near, far, out_rim, agg_rim, d_node_rim, d_nodes1_rim, d_agg_rim = call(
        rim_body,
        [edge, edge, rims, rims, rims, shape(*rims.shape, dtype=F32), rims],
        (nodes, own, near, far, cot, w_node),
        flops=2 * square,
        nbytes=4 * unit,
    )
    far = swapped_across(far, "dom")
    near = swapped(near, "dom", 1)
    halves = [shape(2 * width, width // 2, dtype=F32), shape(2 * width, width // 2)]
    node_parts = call(
        functools.partial(grad_node_body, scale),
        halves if tiled else [shape(2 * width, width)],
        (nodes, agg_mid, agg_rim, d_node_mid, d_node_rim),
        flops=2 * square,
        nbytes=3 * unit,
    )
    if tiled:
        node_parts = (node_parts[0], swapped(node_parts[1], "dp", 1))
    node_out, d_msg, slope = call(
        behind_body,
        [tall, tall_f, tall_f],
        (nodes, adj_t, w_edge, out_mid, out_rim, d_agg_mid, d_agg_rim),
        flops=2 * rows * rows * width + square,
        nbytes=8 * unit,
    )
    back, *g_edge = call(
        functools.partial(edge_body, scale, tiled),
        [shape(ndom, per_peer + 2 * share, width)] if tiled else [shape(ndom, per_peer, width), shape(width, width)],
        (nodes, adj_t, near, far, d_msg, slope, d_nodes1_mid, d_nodes1_rim, w_edge, *(node_parts if tiled else ())),
        scratch=[pltpu.VMEM((rows, width), BF16)],
        flops=2 * square + 4 * rim * rows * width,
        nbytes=8 * unit,
    )
    back = lax.all_to_all(back, "dom", split_axis=0, concat_axis=0, tiled=True)
    if tiled:
        (shared,) = call(share_body, [shape(ndp * ndom, 2 * share, width)], (back,), nbytes=unit)
        shared = lax.all_to_all(shared, ("dp", "dom"), split_axis=0, concat_axis=0, tiled=True)
        grad_edge, grad_node = call(
            finish_body, [shape(width, width, dtype=F32), shape(2 * width, width, dtype=F32)], (shared,), nbytes=2 * unit
        )
    else:
        grad_edge = lax.psum(g_edge[0].astype(F32), ("dp", "dom"))
        grad_node = lax.psum(node_parts[0].astype(F32), ("dp", "dom"))
    (grad_brick,) = call(place_body, [tall], (send_order, back), flops=2 * rows * rows * width, nbytes=2 * unit)
    return (node_out[None], grad_brick[None], grad_edge, grad_node)


def solution(mesh):
    in_specs = (
        P("dp", "dom", None),
        P("dom", None),
        P("dom"),
        P("dom", None),
        P("dom", None, None, None),
        P(),
        P(),
        P("dp", "dom", None),
    )
    out_specs = (P("dp", "dom", None), P("dp", "dom", None), P(), P())
    return jax.shard_map(shards, mesh=mesh, in_specs=in_specs, out_specs=out_specs, check_vma=False)
```

time: 184 us -> 90.7 us (0.49)
  waiting for transfers between devices: 62.8 us -> 26.7 us
  blocking collectives: 52.5 us -> 23 us
  matrix products: 14.8 us -> 0 us
  Pallas kernels: 0 us -> 14.1 us
  between operations: 14.2 us -> 0.78 us
  local copies, waits for them, and re-layouts: 17.8 us -> 6.86 us
  other arithmetic: 6.4 us -> 0 us
  starting transfers between devices: 14.6 us -> 18.7 us
    reduce_scatter x1 -> x0, waiting for transfers between devices: 30.5 us -> none  [shards(): share = lax.psum_scatter(stacked, 'dom', scatter_dimension=0, tiled=True)]
    all_gather x1 -> x0, blocking collectives: 21.6 us -> none  [shards(): whole = lax.all_gather(share, 'dom', axis=0, tiled=True)]
    dot_general x10 -> x0, matrix products: 14.8 us -> none  [the longest x1 4.16 us: shards(): jnp.einsum('wcs,csrh->wrh', table_f, contrib, precision=lax.Precision.HIG...]
    pallas_call x0 -> x11, Pallas kernels: none -> 14.1 us  [call(): pl.pallas_call(body, out_shape=outs, in_specs=specs or [VMEM] * len(args)...]
    ppermute x4 -> x5, waiting for transfers between devices: 17.9 us -> 4.65 us  [the longest x2 3.46 us: swapped_across(): lax.ppermute(x, axis, [(i, (i + 1 if i % 2 else i - 1) % peers) for i in...]
    psum x1 -> x0, blocking collectives: 9.2 us -> none  [shards(): share = lax.psum(share, 'dp')]
    all_to_all x1 -> x2, waiting for transfers between devices: 14.4 us -> 22.1 us  [the longest x1 14.4 us: shards(): lax.all_to_all(shared, ('dp', 'dom'), split_axis=0, concat_axis=0, tiled=...]
    scatter x1 -> x0, local copies, waits for them, and re-layouts: 5.71 us -> none  [shards(): grad_brick = jnp.zeros_like(returned).at[order].set(returned)]
  transfers between devices with their start and end apart: 6 -> 7, of which waited for: 5 -> 5; matrix products, arithmetic and copies ran while one was open for 4% -> 1% of each run, Pallas kernels for 0% -> 8%
where the time goes in v2:
time: 90.7 us; the launch traced here: 90.2 us
  waiting for transfers between devices  26.7 us (29%)
  blocking collectives  23 us (25%)
  starting transfers between devices  18.7 us (21%)
  Pallas kernels  14.1 us (16%)
  local copies, waits for them, and re-layouts  6.86 us (8%)
    all_to_all x1, blocking collectives, shards(): back = lax.all_to_all(back, 'dom', split_axis=0, concat_axis=0, tiled=True)  23 us
    all_to_all x1, waiting for transfers between devices, shards(): lax.all_to_all(shared, ('dp', 'dom'), split_axis=0, concat_axis=0, tiled=...  14.4 us
    pallas_call x11, Pallas kernels, call(): pl.pallas_call(body, out_shape=outs, in_specs=specs or [VMEM] * len(args)...  14.1 us
    all_to_all x1, waiting for transfers between devices, shards(): lax.all_to_all(picked.reshape(ndom, per_peer, width), 'dom', split_axis=0...  7.72 us
    all_to_all x1, starting transfers between devices, shards(): lax.all_to_all(picked.reshape(ndom, per_peer, width), 'dom', split_axis=0...  7.53 us
    unnamed x21, local copies, waits for them, and re-layouts  6.86 us
    ppermute x2, starting transfers between devices, swapped_across(): lax.ppermute(x, axis, [(i, (i + 1 if i % 2 else i - 1) % peers) for i in...  5.63 us
    all_to_all x1, starting transfers between devices, shards(): lax.all_to_all(shared, ('dp', 'dom'), split_axis=0, concat_axis=0, tiled=...  3.82 us
  transfers between devices with their start and end apart: 7, of which 5 were waited for; matrix products, arithmetic and copies ran while one was open for 1% of the time, Pallas kernels for 8%

profile of v2, /device:TPU:0, one launch (start us, length us, event | category | flops | bytes accessed | tf_op | source)
XLA Modules:
  0.0 90.2 jit_solution(3230685804738132221)
XLA Ops:
  0.6 0.0 copy-start.7
  0.6 0.0 copy-start.5
  0.7 2.7 %shard_map.111 = bf16[1024,256]{1,0:T(8,128)(2,1)} custom-call(s32[1,1024]{1,0:T(1,128)} %order_ref.1, bf16[1024,256]{1,0:T(8,128)(2,1)} %bitcast.15), custom_call_target="tpu_custom_call" | custom-call | flops 536870912 | bytes 1048576 | tf_op jit(solution)/shard_map/pallas_call | solution.py:40
  3.4 0.0 copy-start.4
  3.4 0.0 copy-start.6
  3.4 7.5 %all-to-all-start = ((bf16[16,64,256]{2,1,0:T(8,128)(2,1)}), bf16[16,64,256]{2,1,0:T(8,128)(2,1)S(1)}, u32[]{:S(2)}, u32[]{:S(2)}) async-start(bf16[16,64,256]{2,1,0:T(8,128)(2,1)} %bitcast.14), calls=%async_computation | async-start | bytes 1048576 | tf_op jit(solution)/shard_map/all_to_all | solution.py:305
  11.0 0.8 copy.12.tgt_ref
  11.7 0.0 copy-done.7
  11.7 0.0 copy-start.8
  11.7 0.7 copy-done.8
  12.4 1.9 %shard_map.112 = (bf16[13,128,1024]{2,1,0:T(8,128)(2,1)S(1)}, bf16[1024,1664]{1,0:T(8,128)(2,1)S(1)}) custom-call(s32[8]{0:T(128)S(1)} %copy-done.8, s32[8,4]{1,0:T(8,128)S(1)} %copy.12.tgt_ref, bf16[8,4,128,128]{3,2,1,0:T(8,128)(2,1)S(1)} %copy-done.7), custom_call_target="tpu_custom_call" | custom-call | bytes 8388608 | tf_op jit(solution)/shard_map/pallas_call | solution.py:40
  14.2 0.0 copy-start
  14.2 1.7 %copy-done = bf16[1024,1664]{1,0:T(8,128)(2,1)} copy-done((bf16[1024,1664]{1,0:T(8,128)(2,1)}, bf16[1024,1664]{1,0:T(8,128)(2,1)S(1)}, u32[]{:S(2)}) %copy-start) | copy-done | bytes 3407896
  15.9 0.0 copy-start.2
  16.0 1.7 %copy-done.2 = bf16[13,128,1024]{2,1,0:T(8,128)(2,1)} copy-done((bf16[13,128,1024]{2,1,0:T(8,128)(2,1)}, bf16[13,128,1024]{2,1,0:T(8,128)(2,1)S(1)}, u32[]{:S(2)}) %copy-start.2) | copy-done | bytes 3407896
  17.7 7.7 %all-to-all-done = bf16[16,64,256]{2,1,0:T(8,128)(2,1)S(1)} async-done(((bf16[16,64,256]{2,1,0:T(8,128)(2,1)}), bf16[16,64,256]{2,1,0:T(8,128)(2,1)S(1)}, u32[]{:S(2)}, u32[]{:S(2)}) %all-to-all-start) | async-done | bytes 524320 | tf_op jit(solution)/shard_map/all_to_all | solution.py:305
  25.4 0.0 copy-done.5
  25.4 0.0 copy-start.3
  25.4 2.0 %copy-done.3 = bf16[13,128,1024]{2,1,0:T(8,128)(2,1)S(1)} copy-done((bf16[13,128,1024]{2,1,0:T(8,128)(2,1)S(1)}, bf16[13,128,1024]{2,1,0:T(8,128)(2,1)}, u32[]{:S(2)}) %copy-start.3) | copy-done | bytes 3407896
  27.4 0.7 shard_map.113
  28.1 0.1 collective-permute-start
  28.2 2.8 %collective-permute-start.1 = (bf16[256,256]{1,0:T(8,128)(2,1)S(1)}, bf16[256,256]{1,0:T(8,128)(2,1)S(1)}, u32[]{:S(2)}, u32[]{:S(2)}) collective-permute-start(bf16[256,256]{1,0:T(8,128)(2,1)S(1)} %get-tuple-element.35), channel_id=1, source_target_pairs={{0,15},{1,2},{2,1},{3,4},{4,3},{5,6},{6,5},{7,8},{8,7},{9,10},{10,... | collective-permute-start | bytes 393224 | tf_op jit(solution)/shard_map/ppermute | solution.py:28
  31.0 0.0 copy-done.4
  31.0 0.0 copy-done.6
  31.0 0.0 copy-start.1
  31.0 1.5 %shard_map.114 = (bf16[512,256]{1,0:T(8,128)(2,1)S(1)}, bf16[512,256]{1,0:T(8,128)(2,1)S(1)}, bf16[512,256]{1,0:T(8,128)(2,1)S(1)}, bf16[512,256]{1,0:T(8,128)(2...) custom-call(bf16[1024,256]{1,0:T(8,128)(2,1)S(1)} %bitcast.7, ...), custom_call_target="tpu_custom_call" | custom-call | flops 805306368 | bytes 4194304 | tf_op jit(solution)/shard_map/pallas_call | solution.py:40
  32.5 0.0 collective-permute-done.near_in_ref
  32.5 2.8 %collective-permute-done.1.far_in_ref = bf16[256,256]{1,0:T(8,128)(2,1)S(1)} collective-permute-done((bf16[256,256]{1,0:T(8,128)(2,1)S(1)}, bf16[256,256]{1,0:T(8,128)(2,1)S(1)}, u32[]{:S(2)}, u32[]{:S(2)}) %collective-permute-start.1) | collective-permute-done | bytes 131104 | tf_op jit(solution)/shard_map/ppermute | solution.py:28
  35.3 0.7 shard_map.115
  36.0 0.1 collective-permute-start.2
  36.1 2.8 %collective-permute-start.3 = (bf16[256,256]{1,0:T(8,128)(2,1)S(1)}, bf16[256,256]{1,0:T(8,128)(2,1)S(1)}, u32[]{:S(2)}, u32[]{:S(2)}) collective-permute-start(bf16[256,256]{1,0:T(8,128)(2,1)S(1)} %get-tuple-element.41), channel_id=1, source_target_pairs={{0,15},{1,2},{2,1},{3,4},{4,3},{5,6},{6,5},{7,8},{8,7},{9,10},{10,... | collective-permute-start | bytes 393224 | tf_op jit(solution)/shard_map/ppermute | solution.py:28
  38.9 0.5 shard_map.117
  39.4 1.6 %collective-permute-start.4 = (bf16[512,128]{1,0:T(8,128)(2,1)S(1)}, bf16[512,128]{1,0:T(8,128)(2,1)S(1)}, u32[]{:S(2)}, u32[]{:S(2)}) collective-permute-start(bf16[512,128]{1,0:T(8,128)(2,1)S(1)} %get-tuple-element.51), channel_id=1, source_target_pairs={{0,16},{16,0},{1,17},{17,1},{2,18},{18,2},{3,19},{19,3},{4,20},{20... | collective-permute-start | bytes 393224 | tf_op jit(solution)/shard_map/ppermute | solution.py:23
  41.0 0.0 copy-done.1
  41.0 1.6 %shard_map.116 = (bf16[1024,256]{1,0:T(8,128)(2,1)}, f32[1024,256]{1,0:T(8,128)S(1)}, f32[1024,256]{1,0:T(8,128)S(1)}) custom-call(bf16[1024,256]{1,0:T(8,128)(2,1)S(1)} %bitcast.10, bf16[1024,1664]{1,0:T(8,128)(2,1)S(1)} %copy-done.1, bf16[256,256]{1,0:T(8,128)(2,1)S(1)} %copy-done.5, bf16[512,256]{1,0:T(8,128)(2,1)S(1)} %get-tuple-element.32.out_mid_ref, ...), custom_call_target="tpu_custom_call" | custom-call | flops 671088640 | bytes 4194304 | tf_op jit(solution)/shard_map/pallas_call | solution.py:40
  42.6 0.0 collective-permute-done.2.near_ref
  42.6 0.7 collective-permute-done.3.far_ref
  43.2 1.2 %collective-permute-done.4.refs_1_ = bf16[512,128]{1,0:T(8,128)(2,1)S(1)} collective-permute-done((bf16[512,128]{1,0:T(8,128)(2,1)S(1)}, bf16[512,128]{1,0:T(8,128)(2,1)S(1)}, u32[]{:S(2)}, u32[]{:S(2)}) %collective-permute-start.4) | collective-permute-done | bytes 131104 | tf_op jit(solution)/shard_map/ppermute | solution.py:23
  44.4 1.2 %shard_map.118 = bf16[16,96,256]{2,1,0:T(8,128)(2,1)S(1)} custom-call(bf16[1024,256]{1,0:T(8,128)(2,1)S(1)} %bitcast.11, bf16[1024,1664]{1,0:T(8,128)(2,1)S(1)} %copy-done.1, bf16[256,256]{1,0:T(8,128)(2,1)S(1)} %collective-permute-done.2.near_ref, bf16[256,256]{1,0:T(8,128)(2,1)S(1)} %collective-permute-done.3.far_ref, ...), custom_call_target="tpu_custom_call" | custom-call | flops 536870912 | bytes 4194304 | tf_op jit(solution)/shard_map/pallas_call | solution.py:40
  45.7 0.0 copy-start.9
  45.7 23.0 %all_to_all.15.back_ref = bf16[16,96,256]{2,1,0:T(8,128)(2,1)S(1)} all-to-all(bf16[16,96,256]{2,1,0:T(8,128)(2,1)S(1)} %shard_map.118), channel_id=1, replica_groups=mesh['dp'=2,'dom'=16] {'dom'}, dimensions={0} | all-to-all | bytes 1572864 | tf_op jit(solution)/shard_map/all_to_all | solution.py:363
  68.7 0.9 shard_map.120
  69.6 3.8 %all-to-all-start.2 = ((bf16[32,32,256]{2,1,0:T(8,128)(2,1)}), bf16[32,32,256]{2,1,0:T(8,128)(2,1)S(1)}, u32[]{:S(2)}, u32[]{:S(2)}) async-start(bf16[32,32,256]{2,1,0:T(8,128)(2,1)} %shard_map.120), calls=%async_computation.2 | async-start | bytes 1048576 | tf_op jit(solution)/shard_map/all_to_all | solution.py:366
  73.4 0.0 copy-done.9
  73.4 1.5 %shard_map.119 = bf16[1024,256]{1,0:T(8,128)(2,1)} custom-call(s32[1,1024]{1,0:T(1,128)S(1)} %copy-done.9, bf16[16,96,256]{2,1,0:T(8,128)(2,1)S(1)} %all_to_all.15.back_ref), custom_call_target="tpu_custom_call" | custom-call | flops 536870912 | bytes 1048576 | tf_op jit(solution)/shard_map/pallas_call | solution.py:40
  74.9 14.4 %all-to-all-done.2.parts_ref = bf16[32,32,256]{2,1,0:T(8,128)(2,1)S(1)} async-done(((bf16[32,32,256]{2,1,0:T(8,128)(2,1)}), bf16[32,32,256]{2,1,0:T(8,128)(2,1)S(1)}, u32[]{:S(2)}, u32[]{:S(2)}) %all-to-all-start.2) | async-done | bytes 524320 | tf_op jit(solution)/shard_map/all_to_all | solution.py:366
  89.3 0.9 %shard_map.121 = (f32[256,256]{1,0:T(8,128)}, f32[512,256]{1,0:T(8,128)}) custom-call(bf16[32,32,256]{2,1,0:T(8,128)(2,1)S(1)} %all-to-all-done.2.parts_ref), custom_call_target="tpu_custom_call" | custom-call | bytes 1048576 | tf_op jit(solution)/shard_map/pallas_call | solution.py:40
Async XLA Ops:
  0.6 11.1 %copy-start.7 = (bf16[8,4,128,128]{3,2,1,0:T(8,128)(2,1)S(1)}, bf16[8,4,128,128]{3,2,1,0:T(8,128)(2,1)}, u32[]{:S(2)}) copy-start(bf16[8,4,128,128]{3,2,1,0:T(8,128)(2,1)} %vals_ref.1) | copy-start | bytes 3145732
  0.6 24.8 %copy-start.5 = (bf16[256,256]{1,0:T(8,128)(2,1)S(1)}, bf16[256,256]{1,0:T(8,128)(2,1)}, u32[]{:S(2)}) copy-start(bf16[256,256]{1,0:T(8,128)(2,1)} %w_edge_ref.5) | copy-start | bytes 393220
  3.4 27.6 %copy-start.4 = (bf16[1,1024,256]{2,1,0:T(8,128)(2,1)S(1)}, bf16[1,1024,256]{2,1,0:T(8,128)(2,1)}, u32[]{:S(2)}) copy-start(bf16[1,1024,256]{2,1,0:T(8,128)(2,1)} %param.15) | copy-start | bytes 1572868
  3.4 27.6 %copy-start.6 = (bf16[512,256]{1,0:T(8,128)(2,1)S(1)}, bf16[512,256]{1,0:T(8,128)(2,1)}, u32[]{:S(2)}) copy-start(bf16[512,256]{1,0:T(8,128)(2,1)} %w_node_ref.3) | copy-start | bytes 786436
  3.4 22.0 %all-to-all-start = ((bf16[16,64,256]{2,1,0:T(8,128)(2,1)}), bf16[16,64,256]{2,1,0:T(8,128)(2,1)S(1)}, u32[]{:S(2)}, u32[]{:S(2)}) async-start(bf16[16,64,256]{2,1,0:T(8,128)(2,1)} %bitcast.14), calls=%async_computation | async-start | bytes 1048576 | tf_op jit(solution)/shard_map/all_to_all | solution.py:305
  11.7 0.7 copy-start.8
  14.2 1.7 %copy-start = (bf16[1024,1664]{1,0:T(8,128)(2,1)}, bf16[1024,1664]{1,0:T(8,128)(2,1)S(1)}, u32[]{:S(2)}) copy-start(bf16[1024,1664]{1,0:T(8,128)(2,1)S(1)} %get-tuple-element.29.at_ref) | copy-start | bytes 10223620
  15.9 1.7 %copy-start.2 = (bf16[13,128,1024]{2,1,0:T(8,128)(2,1)}, bf16[13,128,1024]{2,1,0:T(8,128)(2,1)S(1)}, u32[]{:S(2)}) copy-start(bf16[13,128,1024]{2,1,0:T(8,128)(2,1)S(1)} %get-tuple-element.30.a_ref) | copy-start | bytes 10223620
  25.4 2.0 %copy-start.3 = (bf16[13,128,1024]{2,1,0:T(8,128)(2,1)S(1)}, bf16[13,128,1024]{2,1,0:T(8,128)(2,1)}, u32[]{:S(2)}) copy-start(bf16[13,128,1024]{2,1,0:T(8,128)(2,1)} %copy-done.2) | copy-start | bytes 10223620
  28.1 4.4 %collective-permute-start = (bf16[256,256]{1,0:T(8,128)(2,1)S(1)}, bf16[256,256]{1,0:T(8,128)(2,1)S(1)}, u32[]{:S(2)}, u32[]{:S(2)}) collective-permute-start(bf16[256,256]{1,0:T(8,128)(2,1)S(1)} %get-tuple-element.34), channel_id=1, source_target_pairs={{0,1},{1,0},{2,3},{3,2},{4,5},{5,4},{6,7},{7,6},{8,9},{9,8},{10,11... | collective-permute-start | bytes 393224 | tf_op jit(solution)/shard_map/ppermute | solution.py:23
  28.2 7.2 %collective-permute-start.1 = (bf16[256,256]{1,0:T(8,128)(2,1)S(1)}, bf16[256,256]{1,0:T(8,128)(2,1)S(1)}, u32[]{:S(2)}, u32[]{:S(2)}) collective-permute-start(bf16[256,256]{1,0:T(8,128)(2,1)S(1)} %get-tuple-element.35), channel_id=1, source_target_pairs={{0,15},{1,2},{2,1},{3,4},{4,3},{5,6},{6,5},{7,8},{8,7},{9,10},{10,... | collective-permute-start | bytes 393224 | tf_op jit(solution)/shard_map/ppermute | solution.py:28
  31.0 10.0 %copy-start.1 = (bf16[1024,1664]{1,0:T(8,128)(2,1)S(1)}, bf16[1024,1664]{1,0:T(8,128)(2,1)}, u32[]{:S(2)}) copy-start(bf16[1024,1664]{1,0:T(8,128)(2,1)} %copy-done) | copy-start | bytes 10223620
  36.0 6.6 %collective-permute-start.2 = (bf16[256,256]{1,0:T(8,128)(2,1)S(1)}, bf16[256,256]{1,0:T(8,128)(2,1)S(1)}, u32[]{:S(2)}, u32[]{:S(2)}) collective-permute-start(bf16[256,256]{1,0:T(8,128)(2,1)S(1)} %get-tuple-element.40), channel_id=1, source_target_pairs={{0,1},{1,0},{2,3},{3,2},{4,5},{5,4},{6,7},{7,6},{8,9},{9,8},{10,11... | collective-permute-start | bytes 393224 | tf_op jit(solution)/shard_map/ppermute | solution.py:23
  36.1 7.2 %collective-permute-start.3 = (bf16[256,256]{1,0:T(8,128)(2,1)S(1)}, bf16[256,256]{1,0:T(8,128)(2,1)S(1)}, u32[]{:S(2)}, u32[]{:S(2)}) collective-permute-start(bf16[256,256]{1,0:T(8,128)(2,1)S(1)} %get-tuple-element.41), channel_id=1, source_target_pairs={{0,15},{1,2},{2,1},{3,4},{4,3},{5,6},{6,5},{7,8},{8,7},{9,10},{10,... | collective-permute-start | bytes 393224 | tf_op jit(solution)/shard_map/ppermute | solution.py:28
  39.4 5.0 %collective-permute-start.4 = (bf16[512,128]{1,0:T(8,128)(2,1)S(1)}, bf16[512,128]{1,0:T(8,128)(2,1)S(1)}, u32[]{:S(2)}, u32[]{:S(2)}) collective-permute-start(bf16[512,128]{1,0:T(8,128)(2,1)S(1)} %get-tuple-element.51), channel_id=1, source_target_pairs={{0,16},{16,0},{1,17},{17,1},{2,18},{18,2},{3,19},{19,3},{4,20},{20... | collective-permute-start | bytes 393224 | tf_op jit(solution)/shard_map/ppermute | solution.py:23
  45.7 27.7 %copy-start.9 = (s32[1,1024]{1,0:T(1,128)S(1)}, s32[1,1024]{1,0:T(1,128)}, u32[]{:S(2)}) copy-start(s32[1,1024]{1,0:T(1,128)} %order_ref.1) | copy-start | bytes 12292
  69.6 19.7 %all-to-all-start.2 = ((bf16[32,32,256]{2,1,0:T(8,128)(2,1)}), bf16[32,32,256]{2,1,0:T(8,128)(2,1)S(1)}, u32[]{:S(2)}, u32[]{:S(2)}) async-start(bf16[32,32,256]{2,1,0:T(8,128)(2,1)} %shard_map.120), calls=%async_computation.2 | async-start | bytes 1048576 | tf_op jit(solution)/shard_map/all_to_all | solution.py:366
